TPU v7x, 32 devices: a whole 2x2x4 slice. The times are simulated.
32 devices in a mesh: ep: 16 (over z, y, x), fsdp: 2 (over core).
Axes of the slice: x: 2, y: 2, z: 4, core: 2. Of those that a mesh axis runs over, the one named last changes fastest.
Arguments:
- tokens: bfloat16 [1536, 4096], P(('ep', 'fsdp')), may hold values from -6 to 6
- expert_ids: int32 [1536, 8], P(('ep', 'fsdp')), may hold values from 0 to 15, all different within a row; in each aligned block of 48 rows (0 to 47, 48 to 95, ...) at most 36 rows name the same one
- gate_values: float32 [1536, 8], P(('ep', 'fsdp')), may hold values from 0.05 to 1
- gate_weight: bfloat16 [16, 4096, 1024], P('ep', None, 'fsdp'), may hold values from -0.09375 to 0.09375
- up_weight: bfloat16 [16, 4096, 1024], P('ep', None, 'fsdp'), may hold values from -0.09375 to 0.09375
- down_weight: bfloat16 [16, 4096, 1024], P('ep', None, 'fsdp'), may hold values from -0.1875 to 0.1875
Outputs:
- mixed: bfloat16 [1536, 4096], P(('ep', 'fsdp'))
Inputs may be any that keep to these rules, and one draw needn't show every extreme that they name: `expert_ids`: each row names 8 different experts. Among the rows of one device's aligned block of 48 tokens no expert is named more than 36 times, and in some blocks one expert is named exactly 36 times.
All inputs are finite; a program needn't handle non-finite values.
Results may differ from a plain program's by a relative error of at most 0.0057.
Values may be sent and summed in bfloat16 or wider, within the bound.
A program may use at most 128 MiB of HBM per device.

v0:
```python
import jax
import jax.numpy as jnp
from jax import lax
from jax.sharding import PartitionSpec as P


def local(tokens, expert_ids, gate_values, gate_weight, up_weight, down_weight):
    tok_rows, model_width = tokens.shape
    top_count = expert_ids.shape[1]
    groups = lax.axis_size("ep")
    capacity = max(2, min(tok_rows, 3 * tok_rows * top_count // (2 * groups)))
    pair_count = tok_rows * top_count
    flat_ids = expert_ids.reshape(pair_count)
    onehot = (flat_ids[:, None] == jnp.arange(groups, dtype=jnp.int32)[None, :]).astype(jnp.int32)
    earlier = jnp.cumsum(onehot, axis=0) - onehot
    slot_index = jnp.sum(earlier * onehot, axis=1)
    position = flat_ids * capacity + slot_index
    source = jnp.repeat(tokens, top_count, axis=0)
    outgoing = jnp.zeros((groups * capacity, model_width), jnp.bfloat16).at[position].set(source)
    outgoing = outgoing.reshape(groups, capacity, model_width)
    gate_shard = gate_weight[0]
    up_shard = up_weight[0]
    down_shard = down_weight[0]
    arrived = lax.all_to_all(outgoing, "ep", split_axis=0, concat_axis=0, tiled=True)
    routed = arrived.reshape(-1, model_width)
    gate_piece = lax.all_gather(gate_shard, "fsdp", axis=1, tiled=True)
    up_piece = lax.all_gather(up_shard, "fsdp", axis=1, tiled=True)
    down_piece = lax.all_gather(down_shard, "fsdp", axis=1, tiled=True)
    gate_part = jnp.dot(routed, gate_piece, preferred_element_type=jnp.float32)
    up_part = jnp.dot(routed, up_piece, preferred_element_type=jnp.float32)
    hidden = (jax.nn.silu(gate_part) * up_part).astype(jnp.bfloat16)
    running = lax.dot_general(
        hidden, down_piece, (((1,), (1,)), ((), ())), preferred_element_type=jnp.float32
    )
    returned = lax.all_to_all(
        running.astype(jnp.bfloat16).reshape(arrived.shape),
        "ep",
        split_axis=0,
        concat_axis=0,
        tiled=True,
    )
    picked = returned.reshape(groups * capacity, model_width)[position]
    weighted = gate_values.reshape(pair_count, 1) * picked.astype(jnp.float32)
    return jnp.sum(weighted.reshape(tok_rows, top_count, model_width), axis=1).astype(jnp.bfloat16)


def solution(mesh):
    placed = (
        P(("ep", "fsdp"), None),
        P(("ep", "fsdp"), None),
        P(("ep", "fsdp"), None),
        P("ep", None, "fsdp"),
        P("ep", None, "fsdp"),
        P("ep", None, "fsdp"),
    )
    return jax.shard_map(
        local, mesh=mesh, in_specs=placed, out_specs=P(("ep", "fsdp"), None), check_vma=False
    )
```

profile of v0, /device:TPU:14, one launch (start us, length us, event | category | flops | bytes accessed | tf_op | source)
XLA Modules:
  0.0 341.2 jit_solution(4313587816982452337)
XLA Ops:
  6.5 0.7 all-gather.9.cloned.1.call-update
  7.3 0.7 all-gather.11.cloned.1.call-update
  8.1 0.1 eq.29
  8.2 0.1 eq.25
  8.3 0.9 reduce-window.6
  9.2 0.2 slice_reduce_fusion
  9.5 0.1 mul.38
  9.6 0.1 fusion.21
  9.7 7.8 %scatter_custom_fusion = bf16[576,4096]{1,0:T(8,128)(2,1)} fusion(s32[384]{0:T(512)S(1)} %fusion.23, bf16[]{:T(256)} %constant.6.clone.1, bf16[48,4096]{1,0:T(8,128)(2,1)S(1)} %copy-done), kind=kCustom, calls=%fused_computation.11 | custom fusion | bytes 5111810 | tf_op jit(solution)/shard_map/scatter | solution.py:19
  17.6 7.8 %reshape.74 = bf16[16,36,4096]{2,1,0:T(8,128)(2,1)} reshape(bf16[576,4096]{1,0:T(8,128)(2,1)} %scatter_custom_fusion) | data formatting | bytes 9437184 | tf_op jit(solution)/shard_map/reshape | solution.py:20
  25.3 7.1 %all-to-all-start = ((bf16[16,36,4096]{2,1,0:T(8,128)(2,1)}), bf16[16,36,4096]{2,1,0:T(8,128)(2,1)}, u32[]{:S(2)}, u32[]{:S(2)}) async-start(bf16[16,36,4096]{2,1,0:T(8,128)(2,1)} %reshape.74), calls=%async_computation | async-start | bytes 10485760 | tf_op jit(solution)/shard_map/all_to_all | solution.py:24
  32.5 0.2 all-gather.7.cloned.1.call-start
  32.7 0.5 all-gather.7.cloned.1.call-update
  33.2 117.2 %all-to-all-done = bf16[16,36,4096]{2,1,0:T(8,128)(2,1)} async-done(((bf16[16,36,4096]{2,1,0:T(8,128)(2,1)}), bf16[16,36,4096]{2,1,0:T(8,128)(2,1)}, u32[]{:S(2)}, u32[]{:S(2)}) %all-to-all-start) | async-done | bytes 4718624 | tf_op jit(solution)/shard_map/all_to_all | solution.py:24
  150.4 7.3 %reshape.75 = bf16[576,4096]{1,0:T(8,128)(2,1)} reshape(bf16[16,36,4096]{2,1,0:T(8,128)(2,1)} %all-to-all-done) | data formatting | bytes 9437184 | tf_op jit(solution)/shard_map/reshape | solution.py:25
  157.7 8.8 %fusion.2 = f32[576,1024]{1,0:T(8,128)S(1)} fusion(bf16[576,4096]{1,0:T(8,128)(2,1)} %reshape.75, bf16[1,4096,1024]{2,1,0:T(8,128)(2,1)} %all-gather.9.cloned.1.call-done), kind=kOutput, calls=%fused_computation.4 | convolution fusion | flops 4831838208 | bytes 15466496 | tf_op jit(solution)/shard_map/dot_general | solution.py:30
  166.6 18.2 %fusion.7 = bf16[576,4096]{1,0:T(8,128)(2,1)} fusion(bf16[1,4096,1024]{2,1,0:T(8,128)(2,1)} %all-gather.11.cloned.1.call-done, f32[576,1024]{1,0:T(8,128)S(1)} %fusion.2, bf16[576,4096]{1,0:T(8,128)(2,1)} %reshape.75, bf16[1,4096,1024]{2,1,0:T(8,128)(2,1)} %all-gather.7.cloned.1.call-done), kind=kOutput, calls=%fused_computation.10 | convolution fusion | flops 9669574656 | bytes 28573696 | tf_op jit(solution)/shard_map/dot_general | solution.py:32
  184.8 7.2 %reshape.76 = bf16[16,36,4096]{2,1,0:T(8,128)(2,1)} reshape(bf16[576,4096]{1,0:T(8,128)(2,1)} %fusion.7) | data formatting | bytes 9437184 | tf_op jit(solution)/shard_map/reshape | solution.py:36
  192.0 5.5 %all-to-all-start.1 = ((bf16[16,36,4096]{2,1,0:T(8,128)(2,1)}), bf16[16,36,4096]{2,1,0:T(8,128)(2,1)}, u32[]{:S(2)}, u32[]{:S(2)}) async-start(bf16[16,36,4096]{2,1,0:T(8,128)(2,1)} %reshape.76), calls=%async_computation.1 | async-start | bytes 10485760 | tf_op jit(solution)/shard_map/all_to_all | solution.py:35
  197.5 0.7 copy.8
  198.2 114.7 %all-to-all-done.1 = bf16[16,36,4096]{2,1,0:T(8,128)(2,1)} async-done(((bf16[16,36,4096]{2,1,0:T(8,128)(2,1)}), bf16[16,36,4096]{2,1,0:T(8,128)(2,1)}, u32[]{:S(2)}, u32[]{:S(2)}) %all-to-all-start.1) | async-done | bytes 4718624 | tf_op jit(solution)/shard_map/all_to_all | solution.py:35
  312.9 7.2 %reshape.77 = bf16[576,4096]{1,0:T(8,128)(2,1)} reshape(bf16[16,36,4096]{2,1,0:T(8,128)(2,1)} %all-to-all-done.1) | data formatting | bytes 9437184 | tf_op jit(solution)/shard_map/reshape | solution.py:42
  320.1 10.5 %gather_fusion = bf16[384,4096]{1,0:T(8,128)(2,1)S(1)} fusion(bf16[576,4096]{1,0:T(8,128)(2,1)} %reshape.77, s32[1024]{0:T(1024)S(1)} %pad_clamp_fusion), kind=kCustom, calls=%fused_computation | custom fusion | bytes 6292992 | tf_op jit(solution)/shard_map/gather | solution.py:42
  330.6 4.1 %fusion.6 = bf16[48,4096]{1,0:T(8,128)(2,1)} fusion(bf16[384,4096]{1,0:T(8,128)(2,1)S(1)} %gather_fusion, f32[48,8]{1,0:T(8,128)} %copy.8), kind=kLoop, calls=%fused_computation.9 | loop fusion | flops 4521984 | bytes 3540480 | tf_op jit(solution)/shard_map/reduce_sum | solution.py:44
  (20 shorter events, 0.3 us)
Async XLA Ops:
  6.5 3.2 copy-start
  6.5 1.5 copy-start.2
  6.5 151.1 %all-gather.9.cloned.1.call-start = ((), (), s32[]{:S(2)}) async-start(), calls=%async_computation.3 | async-start | bytes 12582912 | tf_op jit(solution)/shard_map/all_gather | solution.py:27
  7.3 159.3 %all-gather.11.cloned.1.call-start = ((), (), s32[]{:S(2)}) async-start(), calls=%async_computation.4 | async-start | bytes 12582912 | tf_op jit(solution)/shard_map/all_gather | solution.py:28
  25.3 125.0 %all-to-all-start = ((bf16[16,36,4096]{2,1,0:T(8,128)(2,1)}), bf16[16,36,4096]{2,1,0:T(8,128)(2,1)}, u32[]{:S(2)}, u32[]{:S(2)}) async-start(bf16[16,36,4096]{2,1,0:T(8,128)(2,1)} %reshape.74), calls=%async_computation | async-start | bytes 10485760 | tf_op jit(solution)/shard_map/all_to_all | solution.py:24
  32.5 134.1 %all-gather.7.cloned.1.call-start = ((), (), s32[]{:S(2)}) async-start(), calls=%async_computation.2 | async-start | bytes 12582912 | tf_op jit(solution)/shard_map/all_gather | solution.py:26
  192.0 5.5 %copy-start.3 = (f32[48,8]{0,1:T(8,128)S(1)}, f32[48,8]{0,1:T(8,128)}, u32[]{:S(2)}) copy-start(f32[48,8]{0,1:T(8,128)} %param.8) | copy-start | bytes 4612
  192.0 120.8 %all-to-all-start.1 = ((bf16[16,36,4096]{2,1,0:T(8,128)(2,1)}), bf16[16,36,4096]{2,1,0:T(8,128)(2,1)}, u32[]{:S(2)}, u32[]{:S(2)}) async-start(bf16[16,36,4096]{2,1,0:T(8,128)(2,1)} %reshape.76), calls=%async_computation.1 | async-start | bytes 10485760 | tf_op jit(solution)/shard_map/all_to_all | solution.py:35
  320.1 14.6 %copy-start.1 = (bf16[48,4096]{1,0:T(8,128)(2,1)S(1)}, bf16[48,4096]{1,0:T(8,128)(2,1)}, u32[]{:S(2)}) copy-start(bf16[48,4096]{1,0:T(8,128)(2,1)} %param.6) | copy-start | bytes 1179652
Sparse Core Ops, SparseCore 0:
  8.9 21.2 all-gather.8
  31.7 21.0 all-gather.10
  54.4 21.0 all-gather.6
where the time goes:
time: 342 us; the launch traced here: 341 us
  waiting for transfers between devices  234 us (68%)
  local copies, waits for them, and re-layouts  49.2 us (14%)
  matrix products  27.1 us (8%)
  between operations  13.2 us (4%)
  starting transfers between devices  12.9 us (4%)
  other arithmetic  5.1 us (1%)
    all_to_all x1, waiting for transfers between devices, local(): lax.all_to_all(outgoing, 'ep', split_axis=0, concat_axis=0, tiled=True)  117 us
    all_to_all x1, waiting for transfers between devices, local(): lax.all_to_all(running.astype(jnp.bfloat16).reshape(arrived.shape), 'ep',...  115 us
    dot_general x1, matrix products, local(): lax.dot_general(hidden, down_piece, (((1,), (1,)), ((), ())), preferred_e...  18.2 us
    gather x1, local copies, waits for them, and re-layouts, local(): picked = returned.reshape(groups * capacity, model_width)[position]  10.5 us
    dot_general x1, matrix products, local(): up_part = jnp.dot(routed, up_piece, preferred_element_type=jnp.float32)  8.84 us
    scatter x1, local copies, waits for them, and re-layouts, local(): jnp.zeros((groups * capacity, model_width), jnp.bfloat16).at[position]  7.85 us
    reshape x1, local copies, waits for them, and re-layouts, local(): outgoing = outgoing.reshape(groups, capacity, model_width)  7.76 us
    reshape x1, local copies, waits for them, and re-layouts, local(): routed = arrived.reshape(-1, model_width)  7.27 us
  transfers between devices with their start and end apart: 5, of which 2 were waited for; matrix products, arithmetic and copies ran while one was open for 10% of the time, Pallas kernels for 0%

commit v1 on v0

v1 whole, which is shorter than its diff:
```python
import jax
import jax.numpy as jnp
from jax import lax
from jax.sharding import PartitionSpec as P


def local(tokens, expert_ids, gate_values, gate_weight, up_weight, down_weight):
    groups = lax.axis_size("ep")
    experts = jnp.arange(groups, dtype=jnp.int32)
    chosen = expert_ids[:, :, None] == experts[None, None, :]
    dense_gate = jnp.sum(jnp.where(chosen, gate_values[:, :, None], 0.0), axis=1)
    gates = lax.all_to_all(dense_gate.T, "ep", split_axis=0, concat_axis=0, tiled=True)
    routed = lax.all_gather(tokens, "ep", axis=0, tiled=True)
    gate_piece = lax.all_gather(gate_weight[0], "fsdp", axis=1, tiled=True)
    up_piece = lax.all_gather(up_weight[0], "fsdp", axis=1, tiled=True)
    down_piece = lax.all_gather(down_weight[0], "fsdp", axis=1, tiled=True)
    gate_part = jnp.dot(routed, gate_piece, preferred_element_type=jnp.float32)
    up_part = jnp.dot(routed, up_piece, preferred_element_type=jnp.float32)
    hidden = (jax.nn.silu(gate_part) * up_part).astype(jnp.bfloat16)
    expert_out = lax.dot_general(
        hidden, down_piece, (((1,), (1,)), ((), ())), preferred_element_type=jnp.float32
    ).astype(jnp.bfloat16)
    weighted = (gates.reshape(-1, 1) * expert_out.astype(jnp.float32)).astype(jnp.bfloat16)
    return lax.psum_scatter(weighted, "ep", scatter_dimension=0, tiled=True)


def solution(mesh):
    placed = (
        P(("ep", "fsdp"), None),
        P(("ep", "fsdp"), None),
        P(("ep", "fsdp"), None),
        P("ep", None, "fsdp"),
        P("ep", None, "fsdp"),
        P("ep", None, "fsdp"),
    )
    return jax.shard_map(
        local, mesh=mesh, in_specs=placed, out_specs=P(("ep", "fsdp"), None), check_vma=False
    )
```

time: 342 us -> 336 us (0.982)
  local copies, waits for them, and re-layouts: 49.2 us -> 0.59 us
  waiting for transfers between devices: 234 us -> 274 us
  starting transfers between devices: 12.9 us -> 0.15 us
  blocking collectives: 0 us -> 11.1 us
  matrix products: 27.1 us -> 34.8 us
  other arithmetic: 5.1 us -> 0.7 us
    all_to_all x2 -> x0, waiting for transfers between devices: 232 us -> none  [the longest x1 117 us: local(): lax.all_to_all(outgoing, 'ep', split_axis=0, concat_axis=0, tiled=True)]
    reduce_scatter x0 -> x1, waiting for transfers between devices: none -> 146 us  [local(): return lax.psum_scatter(weighted, 'ep', scatter_dimension=0, tiled=True)]
    all_gather x3 -> x4, waiting for transfers between devices: 0.04 us -> 125 us  [the longest x1 96.3 us: local(): routed = lax.all_gather(tokens, 'ep', axis=0, tiled=True)]
    reshape x4 -> x0, local copies, waits for them, and re-layouts: 29.5 us -> none  [the longest x1 7.76 us: local(): outgoing = outgoing.reshape(groups, capacity, model_width)]
    all_to_all x2 -> x0, starting transfers between devices: 12.6 us -> none  [the longest x1 7.12 us: local(): lax.all_to_all(outgoing, 'ep', split_axis=0, concat_axis=0, tiled=True)]
    dot_general x0 -> x1, matrix products: none -> 12.5 us  [local(): gate_part = jnp.dot(routed, gate_piece, preferred_element_type=jnp.float32)]
    all_to_all x0 -> x1, blocking collectives: none -> 11.1 us  [local(): lax.all_to_all(dense_gate.T, 'ep', split_axis=0, concat_axis=0, tiled=True)]
    gather x1 -> x0, local copies, waits for them, and re-layouts: 10.5 us -> none  [local(): picked = returned.reshape(groups * capacity, model_width)[position]]
  transfers between devices with their start and end apart: 5 -> 5, of which waited for: 2 -> 5; matrix products, arithmetic and copies ran while one was open for 10% -> 7% of each run, Pallas kernels for 0% -> 0%
where the time goes in v1:
time: 336 us; the launch traced here: 334 us
  waiting for transfers between devices  274 us (82%)
  matrix products  34.8 us (10%)
  between operations  13.2 us (4%)
  blocking collectives  11.1 us (3%)
    reduce_scatter x1, waiting for transfers between devices, local(): return lax.psum_scatter(weighted, 'ep', scatter_dimension=0, tiled=True)  146 us
    all_gather x1, waiting for transfers between devices, local(): routed = lax.all_gather(tokens, 'ep', axis=0, tiled=True)  96.3 us
    dot_general x1, matrix products, local(): gate_part = jnp.dot(routed, gate_piece, preferred_element_type=jnp.float32)  12.5 us
    dot_general x1, matrix products, local(): lax.dot_general(hidden, down_piece, (((1,), (1,)), ((), ())), preferred_e...  11.4 us
    all_to_all x1, blocking collectives, local(): lax.all_to_all(dense_gate.T, 'ep', split_axis=0, concat_axis=0, tiled=True)  11.1 us
    dot_general x1, matrix products, local(): up_part = jnp.dot(routed, up_piece, preferred_element_type=jnp.float32)  10.9 us
    all_gather x1, waiting for transfers between devices, local(): gate_piece = lax.all_gather(gate_weight[0], 'fsdp', axis=1, tiled=True)  10.6 us
    all_gather x1, waiting for transfers between devices, local(): down_piece = lax.all_gather(down_weight[0], 'fsdp', axis=1, tiled=True)  9.96 us
  transfers between devices with their start and end apart: 5, of which 5 were waited for; matrix products, arithmetic and copies ran while one was open for 7% of the time, Pallas kernels for 0%

profile of v1, /device:TPU:14, one launch (start us, length us, event | category | flops | bytes accessed | tf_op | source)
XLA Modules:
  0.0 334.3 jit_solution(6434408792974554575)
XLA Ops:
  6.5 0.0 all-gather.12.cloned.1.call-start
  6.5 0.7 all-gather.12.cloned.1.call-update
  7.3 0.0 all-gather.8.cloned.1.call-start
  7.3 0.7 all-gather.8.cloned.1.call-update
  8.0 0.0 all-gather.10.cloned.1.call-start
  8.1 0.7 all-gather.10.cloned.1.call-update
  8.7 0.0 all-gather.14.cloned.1.call-start
  8.8 0.5 all-gather.14.cloned.1.call-update
  9.3 0.0 reduce-scatter.2.cloned.1.call-start
  9.4 0.0 copy-done.1
  9.4 0.0 copy-done
  9.4 11.1 %all_to_all.9 = f32[16,1,48]{2,1,0:T(1,128)S(1)} all-to-all(f32[16,1,48]{2,1,0:T(1,128)S(1)} %bitcast.23), channel_id=1, replica_groups=mesh['ep'=16,'fsdp'=2] {'ep'}, dimensions={0} | all-to-all | bytes 6144 | tf_op jit(solution)/shard_map/all_to_all | solution.py:12
  20.5 0.5 broadcast.7
  21.0 0.7 reduce.3
  21.7 0.1 mul.17
  21.8 8.4 %all-gather.12.cloned.1.call-done = bf16[1,4096,1024]{2,1,0:T(8,128)(2,1)} async-done(((bf16[1,4096,512]{2,1,0:T(8,128)(2,1)}), bf16[1,4096,1024]{2,1,0:T(8,128)(2,1)}) %all-gather.12.cloned.1.call-update) | async-done | bytes 8388624 | tf_op jit(solution)/shard_map/all_gather | solution.py:15
  30.1 96.3 %all-gather.8.cloned.1.call-done = bf16[768,4096]{1,0:T(8,128)(2,1)} async-done(((bf16[48,4096]{1,0:T(8,128)(2,1)}), bf16[768,4096]{1,0:T(8,128)(2,1)}) %all-gather.8.cloned.1.call-update) | async-done | bytes 6291472 | tf_op jit(solution)/shard_map/all_gather | solution.py:13
  126.4 10.9 %fusion.2 = f32[768,1024]{1,0:T(8,128)S(1)} fusion(bf16[768,4096]{1,0:T(8,128)(2,1)} %all-gather.8.cloned.1.call-done, bf16[1,4096,1024]{2,1,0:T(8,128)(2,1)} %all-gather.12.cloned.1.call-done), kind=kOutput, calls=%fused_computation.3 | convolution fusion | flops 6442450944 | bytes 17825792 | tf_op jit(solution)/shard_map/dot_general | solution.py:18
  137.4 10.6 %all-gather.10.cloned.1.call-done = bf16[1,4096,1024]{2,1,0:T(8,128)(2,1)} async-done(((bf16[1,4096,512]{2,1,0:T(8,128)(2,1)}), bf16[1,4096,1024]{2,1,0:T(8,128)(2,1)}) %all-gather.10.cloned.1.call-update) | async-done | bytes 8388624 | tf_op jit(solution)/shard_map/all_gather | solution.py:14
  148.0 12.5 %multiply_convert_fusion.1 = bf16[768,1024]{1,0:T(8,128)(2,1)} fusion(f32[768,1024]{1,0:T(8,128)S(1)} %fusion.2, bf16[768,4096]{1,0:T(8,128)(2,1)} %all-gather.8.cloned.1.call-done, bf16[1,4096,1024]{2,1,0:T(8,128)(2,1)} %all-gather.10.cloned.1.call-done), kind=kOutput, calls=%fused_computation.8 | convolution fusion | flops 6447169536 | bytes 19398656 | tf_op jit(solution)/shard_map/dot_general | solution.py:17
  160.5 10.0 %all-gather.14.cloned.1.call-done = bf16[1,4096,1024]{2,1,0:T(8,128)(2,1)} async-done(((bf16[1,4096,512]{2,1,0:T(8,128)(2,1)}), bf16[1,4096,1024]{2,1,0:T(8,128)(2,1)}) %all-gather.14.cloned.1.call-update) | async-done | bytes 8388624 | tf_op jit(solution)/shard_map/all_gather | solution.py:16
  170.4 11.4 %multiply_convert_fusion = bf16[768,4096]{1,0:T(8,128)(2,1)} fusion(bf16[768,1024]{1,0:T(8,128)(2,1)} %multiply_convert_fusion.1, bf16[1,4096,1024]{2,1,0:T(8,128)(2,1)} %all-gather.14.cloned.1.call-done, f32[768]{0:T(1024)S(1)} %mul.17), kind=kOutput, calls=%fused_computation | convolution fusion | flops 6455033856 | bytes 16256000 | tf_op jit(solution)/shard_map/dot_general | solution.py:20
  181.8 0.0 reduce-scatter.2.cloned.1.call-update
  181.8 145.9 %reduce-scatter.2.cloned.1.call-done = bf16[48,4096]{1,0:T(8,128)(2,1)} async-done(((bf16[768,4096]{1,0:T(8,128)(2,1)}), bf16[48,4096]{1,0:T(8,128)(2,1)}) %reduce-scatter.2.cloned.1.call-update) | async-done | bytes 393232 | tf_op jit(solution)/shard_map/reduce_scatter | solution.py:24
  (3 shorter events, 0.0 us)
Async XLA Ops:
  6.5 2.8 copy-start.1
  6.5 2.8 copy-start
  6.5 23.6 %all-gather.12.cloned.1.call-start = ((), (), s32[]{:S(2)}) async-start(), calls=%async_computation.5 | async-start | bytes 12582912 | tf_op jit(solution)/shard_map/all_gather | solution.py:15
  7.3 119.2 %all-gather.8.cloned.1.call-start = ((), (), s32[]{:S(2)}) async-start(), calls=%async_computation.2 | async-start | bytes 6684672 | tf_op jit(solution)/shard_map/all_gather | solution.py:13
  8.0 140.0 %all-gather.10.cloned.1.call-start = ((), (), s32[]{:S(2)}) async-start(), calls=%async_computation.4 | async-start | bytes 12582912 | tf_op jit(solution)/shard_map/all_gather | solution.py:14
  8.7 161.7 %all-gather.14.cloned.1.call-start = ((), (), s32[]{:S(2)}) async-start(), calls=%async_computation.6 | async-start | bytes 12582912 | tf_op jit(solution)/shard_map/all_gather | solution.py:16
  9.3 318.4 %reduce-scatter.2.cloned.1.call-start = ((), (), s32[]{:S(2)}) async-start(), calls=%async_computation.3 | async-start | bytes 6684672 | tf_op jit(solution)/shard_map/reduce_scatter | solution.py:24
Sparse Core Ops, SparseCore 0:
  8.9 21.1 all-gather.11
  32.9 93.4 all-gather.7
  128.0 19.9 all-gather.9
  149.4 21.0 all-gather.13
  181.9 145.7 reduce-scatter.1

commit v2 on v1

--- a/solution.py
+++ b/solution.py
@@ -1,10 +1,19 @@
+import functools
+import math
+
 import jax
 import jax.numpy as jnp
 from jax import lax
+from jax.experimental import pallas as pl
+from jax.experimental.pallas import tpu as pltpu
 from jax.sharding import PartitionSpec as P
 
-
-def local(tokens, expert_ids, gate_values, gate_weight, up_weight, down_weight):
+MESH = pl.DeviceIdType.MESH
+VMEM_LIMIT = 60 * 1024 * 1024
+LANES = 128
+
+
+def plain(tokens, expert_ids, gate_values, gate_weight, up_weight, down_weight):
     groups = lax.axis_size("ep")
     experts = jnp.arange(groups, dtype=jnp.int32)
     chosen = expert_ids[:, :, None] == experts[None, None, :]
@@ -24,6 +33,277 @@
     return lax.psum_scatter(weighted, "ep", scatter_dimension=0, tiled=True)
 
 
+def flip(index, mask):
+    bit = 1
+    while bit <= mask:
+        if mask & bit:
+            index = index + bit * (1 - 2 * ((index // bit) % 2))
+        bit *= 2
+    return index
+
+
+def kernel(
+    groups, rows, width, units, top, pieces,
+    tokens_ref, ids_ref, values_ref, gate_hbm, up_hbm, down_hbm, out_ref,
+    tok, wg, wu, wd, hid, part, relay_x, relay_y, from_x, from_y, plane_sum, from_z,
+    local_sem, send_sem, recv_sem,
+):
+    me = lax.axis_index("ep")
+    core = lax.axis_index("fsdp")
+    planes = list(range(0, groups, 4))
+    half = width // 2
+    counter = [0]
+
+    def peer(mask):
+        return (flip(me, mask), core)
+
+    def remote(src, dst, device):
+        number = counter[0]
+        counter[0] += 1
+        return pltpu.make_async_remote_copy(
+            src_ref=src, dst_ref=dst, send_sem=send_sem.at[number], recv_sem=recv_sem.at[number],
+            device_id=device, device_id_type=MESH,
+        )
+
+    def slot(ref, mask):
+        return ref.at[pl.ds(mask * rows, rows)]
+
+    def left(ref, mask):
+        return ref.at[pl.ds(mask * rows, rows), pl.ds(0, half)]
+
+    def right(ref, mask, total):
+        return ref.at[pl.ds(mask * rows, rows), pl.ds(half, total - half)]
+
+    full = width + LANES
+    ends = {p: remote(slot(tok, 0), slot(tok, p), peer(p)) for p in planes[1:]}
+    whole_x = {p: remote(slot(tok, p), slot(tok, p + 1), peer(1)) for p in planes}
+    whole_y = {p: remote(slot(tok, p), slot(tok, p + 2), peer(2)) for p in planes}
+    on_y = {p: remote(left(tok, p + 1), left(tok, p + 3), peer(2)) for p in planes}
+    on_x = {p: remote(right(tok, p + 2, full), right(tok, p + 3, full), peer(1)) for p in planes}
+    sibling = (me, flip(core, 1))
+    other = [
+        remote(gate_hbm.at[0], wg.at[1], sibling),
+        remote(up_hbm.at[0], wu.at[1], sibling),
+        remote(down_hbm.at[0], wd.at[1], sibling),
+    ]
+    diag_x, diag_y, sum_x, sum_y, sum_z = {}, {}, {}, {}, {}
+    for i, p in enumerate(planes):
+        diag_x[p] = remote(left(part, p + 3), slot(relay_x, i), peer(1))
+        diag_y[p] = remote(right(part, p + 3, width), slot(relay_y, i), peer(2))
+        sum_x[p] = remote(slot(part, p + 1), slot(from_x, i), peer(1))
+        sum_y[p] = remote(slot(part, p + 2), slot(from_y, i), peer(2))
+        if i:
+            sum_z[p] = remote(slot(plane_sum, i), slot(from_z, i - 1), peer(p))
+
+    barrier = pltpu.get_barrier_semaphore()
+    for mask in [1, 2] + planes[1:]:
+        pl.semaphore_signal(barrier, inc=1, device_id=peer(mask), device_id_type=MESH)
+    pl.semaphore_signal(barrier, inc=1, device_id=sibling, device_id_type=MESH)
+
+    own = [
+        pltpu.make_async_copy(gate_hbm.at[0], wg.at[0], local_sem.at[0]),
+        pltpu.make_async_copy(up_hbm.at[0], wu.at[0], local_sem.at[1]),
+        pltpu.make_async_copy(down_hbm.at[0], wd.at[0], local_sem.at[2]),
+    ]
+    mine = pltpu.make_async_copy(tokens_ref, tok.at[pl.ds(0, rows), pl.ds(0, width)], local_sem.at[3])
+    mine.start()
+    for copy in own:
+        copy.start()
+
+    lane = lax.broadcasted_iota(jnp.int32, (rows, LANES), 1)
+    expert = lane % groups
+    dense = jnp.zeros((rows, LANES), jnp.float32)
+    for k in range(top):
+        dense = dense + jnp.where(ids_ref[:, k:k + 1] == expert, values_ref[:, k:k + 1], 0.0)
+    piece = lane // groups
+    packed, rest = jnp.zeros((rows, LANES), jnp.float32), dense
+    for i in range(pieces):
+        rounded = rest.astype(jnp.bfloat16).astype(jnp.float32)
+        packed = jnp.where(piece == i, rounded, packed)
+        rest = rest - rounded
+    tok[0:rows, width:full] = packed.astype(jnp.bfloat16)
+
+    mine.wait()
+    pl.semaphore_wait(barrier, 2 + len(planes))
+
+    for p in planes[1:3]:
+        ends[p].start()
+    whole_x[0].start()
+    whole_y[0].start()
+    for copy in other:
+        copy.start()
+
+    block = 4 * rows
+    step = math.gcd(units, 256)
+
+    def gate_up(p, h):
+        def body(j, carry):
+            columns = pl.ds(pl.multiple_of(j * step, step), step)
+            x = tok[p * rows:p * rows + block, 0:width]
+            g = jnp.dot(x, wg[h, :, columns], preferred_element_type=jnp.float32)
+            u = jnp.dot(x, wu[h, :, columns], preferred_element_type=jnp.float32)
+            hid[h, :, columns] = (g / (1.0 + jnp.exp(-g)) * u).astype(jnp.bfloat16)
+            return carry
+
+        lax.fori_loop(0, units // step, body, 0)
+
+    def down(p):
+        lanes = lax.broadcasted_iota(jnp.int32, (block, LANES), 1)
+        shown = tok[p * rows:p * rows + block, width:full].astype(jnp.float32)
+        gate = jnp.sum(jnp.where(lanes % groups == me, shown, 0.0), axis=1, keepdims=True)
+        wide = math.gcd(width, 512)
+
+        def body(n, carry):
+            features = pl.ds(pl.multiple_of(n * wide, wide), wide)
+            total = None
+            for h in range(2):
+                term = lax.dot_general(
+                    hid[h], wd[h, features, :], (((1,), (1,)), ((), ())),
+                    preferred_element_type=jnp.float32,
+                )
+                total = term if total is None else total + term
+            rounded = total.astype(jnp.bfloat16).astype(jnp.float32)
+            part[p * rows:p * rows + block, features] = (gate * rounded).astype(jnp.bfloat16)
+            return carry
+
+        lax.fori_loop(0, width // wide, body, 0)
+
+    def add_relays(p):
+        i = p // 4
+        here = slice(i * rows, (i + 1) * rows)
+        diag_x[p].wait_recv()
+        diag_y[p].wait_recv()
+        to_y = slice((p + 2) * rows, (p + 3) * rows)
+        to_x = slice((p + 1) * rows, (p + 2) * rows)
+        part[to_y, 0:half] = (
+            part[to_y, 0:half].astype(jnp.float32) + relay_x[here].astype(jnp.float32)
+        ).astype(jnp.bfloat16)
+        part[to_x, half:width] = (
+            part[to_x, half:width].astype(jnp.float32) + relay_y[here].astype(jnp.float32)
+        ).astype(jnp.bfloat16)
+        sum_x[p].start()
+        sum_y[p].start()
+
+    def finish_plane(p):
+        i = p // 4
+        here = slice(i * rows, (i + 1) * rows)
+        sum_x[p].wait_recv()
+        sum_y[p].wait_recv()
+        total = (
+            part[p * rows:(p + 1) * rows].astype(jnp.float32)
+            + from_x[here].astype(jnp.float32)
+            + from_y[here].astype(jnp.float32)
+        )
+        if i:
+            plane_sum[here] = total.astype(jnp.bfloat16)
+            sum_z[p].start()
+        return total
+
+    order = []
+    for i, p in enumerate(planes):
+        whole_x[p].wait_recv()
+        on_y[p].start()
+        whole_y[p].wait_recv()
+        on_x[p].start()
+        if i == 0:
+            for q in planes[3:]:
+                ends[q].start()
+        if i + 1 < len(planes):
+            following = planes[i + 1]
+            ends[following].wait_recv()
+            whole_x[following].start()
+            whole_y[following].start()
+        on_y[p].wait_recv()
+        on_x[p].wait_recv()
+        if i == 0:
+            own[0].wait()
+            own[1].wait()
+        gate_up(p, 0)
+        if i == 0:
+            other[0].wait_recv()
+            other[1].wait_recv()
+        gate_up(p, 1)
+        if i == 0:
+            own[2].wait()
+            other[2].wait_recv()
+        down(p)
+        if i:
+            diag_x[p].start()
+            diag_y[p].start()
+            order.append(p)
+        if len(order) >= 2:
+            add_relays(order[-2])
+        if len(order) >= 3:
+            finish_plane(order[-3])
+    diag_x[0].start()
+    diag_y[0].start()
+    order.append(0)
+    count = len(order)
+    finish_plane(order[count - 3])
+    add_relays(order[count - 2])
+    add_relays(order[count - 1])
+    finish_plane(order[count - 2])
+    total = finish_plane(order[count - 1])
+    for i, p in enumerate(planes[1:]):
+        sum_z[p].wait_recv()
+        total = total + from_z[i * rows:(i + 1) * rows].astype(jnp.float32)
+    out_ref[...] = total.astype(jnp.bfloat16)
+
+    for group in (ends, whole_x, whole_y, on_y, on_x, diag_x, diag_y, sum_x, sum_y, sum_z):
+        for copy in group.values():
+            copy.wait_send()
+    for copy in other:
+        copy.wait_send()
+
+
+def fused(tokens, expert_ids, gate_values, gate_weight, up_weight, down_weight):
+    rows, width = tokens.shape
+    units = gate_weight.shape[2]
+    top = expert_ids.shape[1]
+    groups = lax.axis_size("ep")
+    planes = groups // 4
+    half = width // 2
+    copies = 3 + (planes - 1) * 2 + planes * 8
+    bf16 = jnp.bfloat16
+    run = pl.pallas_call(
+        functools.partial(kernel, groups, rows, width, units, top, 3),
+        out_shape=jax.ShapeDtypeStruct((rows, width), bf16),
+        in_specs=[
+            pl.BlockSpec(memory_space=pl.ANY),
+            pl.BlockSpec(memory_space=pltpu.VMEM),
+            pl.BlockSpec(memory_space=pltpu.VMEM),
+            pl.BlockSpec(memory_space=pl.ANY),
+            pl.BlockSpec(memory_space=pl.ANY),
+            pl.BlockSpec(memory_space=pl.ANY),
+        ],
+        out_specs=pl.BlockSpec(memory_space=pltpu.VMEM),
+        scratch_shapes=[
+            pltpu.VMEM((groups * rows, width + LANES), bf16),
+            pltpu.VMEM((2, width, units), bf16),
+            pltpu.VMEM((2, width, units), bf16),
+            pltpu.VMEM((2, width, units), bf16),
+            pltpu.VMEM((2, 4 * rows, units), bf16),
+            pltpu.VMEM((groups * rows, width), bf16),
+            pltpu.VMEM((planes * rows, half), bf16),
+            pltpu.VMEM((planes * rows, width - half), bf16),
+            pltpu.VMEM((planes * rows, width), bf16),
+            pltpu.VMEM((planes * rows, width), bf16),
+            pltpu.VMEM((planes * rows, width), bf16),
+            pltpu.VMEM(((planes - 1) * rows, width), bf16),
+            pltpu.SemaphoreType.DMA((4,)),
+            pltpu.SemaphoreType.DMA((copies,)),
+            pltpu.SemaphoreType.DMA((copies,)),
+        ],
+        compiler_params=pltpu.CompilerParams(
+            collective_id=0, has_side_effects=True, vmem_limit_bytes=VMEM_LIMIT
+        ),
+        cost_estimate=pl.CostEstimate(
+            flops=12 * groups * rows * width * units, bytes_accessed=6 * width * units, transcendentals=0
+        ),
+    )
+    return run(tokens, expert_ids, gate_values, gate_weight, up_weight, down_weight)
+
+
 def solution(mesh):
     placed = (
         P(("ep", "fsdp"), None),
@@ -33,6 +313,21 @@
         P("ep", None, "fsdp"),
         P("ep", None, "fsdp"),
     )
+    groups, cores = mesh.shape["ep"], mesh.shape["fsdp"]
+
+    def local(tokens, expert_ids, gate_values, gate_weight, up_weight, down_weight):
+        rows, width = tokens.shape
+        units = gate_weight.shape[2]
+        held = 2 * (6 * width * units + 4 * rows * 2 * units)
+        held += 2 * rows * width * (2 * groups + groups)
+        fits = held + VMEM_LIMIT // 6 <= VMEM_LIMIT
+        shaped = (
+            cores == 2 and groups >= 16 and groups & (groups - 1) == 0 and 3 * groups <= LANES
+            and rows % 16 == 0 and width % 256 == 0 and units % 128 == 0
+        )
+        part = fused if fits and shaped else plain
+        return part(tokens, expert_ids, gate_values, gate_weight, up_weight, down_weight)
+
     return jax.shard_map(
         local, mesh=mesh, in_specs=placed, out_specs=P(("ep", "fsdp"), None), check_vma=False
     )

time: 336 us -> 134 us (0.40)
  waiting for transfers between devices: 274 us -> 0 us
  Pallas kernels: 0 us -> 128 us
  matrix products: 34.8 us -> 0 us
  between operations: 13.2 us -> 0.01 us
  blocking collectives: 11.1 us -> 0 us
  local copies, waits for them, and re-layouts: 0.59 us -> 4.5 us
    reduce_scatter x1 -> x0, waiting for transfers between devices: 146 us -> none  [local(): return lax.psum_scatter(weighted, 'ep', scatter_dimension=0, tiled=True)]
    pallas_call x0 -> x1, Pallas kernels: none -> 128 us  [fused(): run(tokens, expert_ids, gate_values, gate_weight, up_weight, down_weight)]
    all_gather x4 -> x0, waiting for transfers between devices: 125 us -> none  [the longest x1 96.3 us: local(): routed = lax.all_gather(tokens, 'ep', axis=0, tiled=True)]
    dot_general x3 -> x0, matrix products: 34.8 us -> none  [the longest x1 12.5 us: local(): gate_part = jnp.dot(routed, gate_piece, preferred_element_type=jnp.float32)]
    all_to_all x1 -> x0, blocking collectives: 11.1 us -> none  [local(): lax.all_to_all(dense_gate.T, 'ep', split_axis=0, concat_axis=0, tiled=True)]
    unnamed x4 -> x3, local copies, waits for them, and re-layouts: 0.01 us -> 4.5 us
  transfers between devices with their start and end apart: 5 -> 0, of which waited for: 5 -> 0; matrix products, arithmetic and copies ran while one was open for 7% -> 0% of each run, Pallas kernels for 0% -> 0%
where the time goes in v2:
time: 134 us; the launch traced here: 132 us
  Pallas kernels  128 us (96%)
  local copies, waits for them, and re-layouts  4.5 us (3%)
    pallas_call x1, Pallas kernels, fused(): run(tokens, expert_ids, gate_values, gate_weight, up_weight, down_weight)  128 us
    unnamed x3, local copies, waits for them, and re-layouts  4.5 us

profile of v2, /device:TPU:14, one launch (start us, length us, event | category | flops | bytes accessed | tf_op | source)
XLA Modules:
  0.0 132.3 jit_solution(3789773705163286144)
XLA Ops:
  0.0 1.4 %copy.7.ids_ref = s32[48,8]{1,0:T(8,128)} copy(s32[48,8]{0,1:T(8,128)} %param.7) | data formatting | bytes 3072 | tf_op args[1]
  1.4 1.4 %copy.8.values_ref = f32[48,8]{1,0:T(8,128)} copy(f32[48,8]{0,1:T(8,128)} %param.8) | data formatting | bytes 3072 | tf_op args[2]
  2.7 127.8 %shard_map.64 = bf16[48,4096]{1,0:T(8,128)(2,1)} custom-call(bf16[48,4096]{1,0:T(8,128)(2,1)} %tokens_ref.1, s32[48,8]{1,0:T(8,128)} %copy.7.ids_ref, f32[48,8]{1,0:T(8,128)} %copy.8.values_ref, bf16[1,4096,512]{2,1,0:T(8,128)(2,1)} %gate_hbm.1, bf16[1,4096,512]{2,1,0:T(8,128)(2,1)} %up_hbm.1, bf16[1,4096,512]{2,1,0:T(8,128)(2,1)} %down_hbm.1), custom_call_target="tpu_custom_call" | custom-call | flops 19327352832 | bytes 12582912 | tf_op jit(solution)/shard_map/pallas_call | solution.py:304
  130.6 1.8 %copy.10 = bf16[48,4096]{1,0:T(8,128)(2,1)} copy(bf16[48,4096]{1,0:T(8,128)(2,1)} %shard_map.64) | data formatting | bytes 786432
